TPU v7x, 32 devices: a whole 2x2x4 slice. The times are simulated.
32 devices in a mesh: rep: 4 (over y, core), sp: 8 (over z, x).
Axes of the slice: x: 2, y: 2, z: 4, core: 2. Of those that a mesh axis runs over, the one named last changes fastest.
Arguments:
- queries: bfloat16 [8192, 8192], P(('rep', 'sp')), may hold values from -12 to 12
- keys: bfloat16 [8192, 1024], P(('rep', 'sp')), may hold values from -12 to 12
- values: bfloat16 [8192, 1024], P(('rep', 'sp')), may hold values from -6 to 6
- doc_lengths: int32 [4, 16], P('rep'), may hold values from 1 to 512, 2048 in all within a row
- dest_group: int32 [4, 64], replicated, may hold values from 0 to 3, as said below
- dest_slot: int32 [4, 64], replicated, may hold values from 0 to 7, as said below
Outputs:
- attended: bfloat16 [8192, 8192], P(('rep', 'sp'))
Inputs may be any that keep to these rules, and one draw needn't show every extreme that they name: Piece j of sp index s of group g goes to the same sp index of group dest_group[g, s * 8 + j]; the 8 pieces of each device go to exactly half of the 4 groups, 4 to each. `dest_slot`: on every device of every group each of the 8 slots receives exactly one piece.
All inputs are finite; a program needn't handle non-finite values.
Results may differ from a plain program's by a relative error of at most 0.004.
Values may be sent and summed in bfloat16 or wider, within the bound.
A program may use at most 192 MiB of HBM per device.

v0:
```python
import math

import jax
import jax.numpy as jnp
from jax import lax
from jax.sharding import PartitionSpec as P

QUERY_HEADS = 64
KEY_VALUE_HEADS = 8
HEAD_WIDTH = 128
DEVICE_PIECES = 8
TILE_ROWS = 512
PIECE_LENGTH = 32


MASKED = -1e30


def doc_starts(positions, lengths):
    doc_ends = jnp.cumsum(lengths)
    return jnp.sum(jnp.where(positions[:, None] >= doc_ends[None, :], lengths[None, :], 0), axis=1)


def route_ranks(dest_group, group_total, device_count):
    groups_all = dest_group.reshape(group_total, device_count, DEVICE_PIECES)
    earlier = jnp.arange(DEVICE_PIECES)[:, None] > jnp.arange(DEVICE_PIECES)[None, :]
    same_target = groups_all[:, :, :, None] == groups_all[:, :, None, :]
    order_rank = jnp.sum((same_target & earlier[None, None]).astype(jnp.int32), axis=3)
    return (groups_all, order_rank)


def send_table(groups_all, order_rank, group_self, shard_self, group_total, capacity):
    target_self = groups_all[group_self, shard_self]
    rank_self = order_rank[group_self, shard_self]
    chosen = (target_self[None, None, :] == jnp.arange(group_total)[:, None, None]) & (
        rank_self[None, None, :] == jnp.arange(capacity)[None, :, None]
    )
    return chosen.astype(jnp.bfloat16)


def receive_table(groups_all, order_rank, slots_all, group_self, capacity):
    arrived = (groups_all == group_self).astype(jnp.float32)
    rank_onehot = (order_rank[..., None] == jnp.arange(capacity)).astype(jnp.float32)
    slot_onehot = (slots_all[..., None] == jnp.arange(DEVICE_PIECES)).astype(jnp.float32)
    return jnp.einsum("gtj,gtjc,gtjz->tzgc", arrived, rank_onehot, slot_onehot).astype(jnp.bfloat16)


def arrange(table, arrived_rows, form):
    return jnp.einsum(form, table, arrived_rows, preferred_element_type=jnp.float32).astype(
        jnp.bfloat16
    )


def heads_attention(stream_query, stream_key, stream_value, starts, score_scale):
    stream_rows = stream_query.shape[0]
    head_count = stream_query.shape[1]

    def one_block(block_index):
        row_begin = block_index * TILE_ROWS
        query_block_rows = lax.dynamic_slice_in_dim(stream_query, row_begin, TILE_ROWS, 0)
        query_starts = lax.dynamic_slice_in_dim(starts, row_begin, TILE_ROWS, 0)
        query_positions = row_begin + jnp.arange(TILE_ROWS)

        def add_block(key_index, carry):
            running_max, running_sum, running_out = carry
            key_first = key_index * TILE_ROWS
            key_block_rows = lax.dynamic_slice_in_dim(stream_key, key_first, TILE_ROWS, 0)
            value_block_rows = lax.dynamic_slice_in_dim(stream_value, key_first, TILE_ROWS, 0)
            key_starts = lax.dynamic_slice_in_dim(starts, key_first, TILE_ROWS, 0)
            key_positions = key_first + jnp.arange(TILE_ROWS)
            scores = (
                jnp.einsum(
                    "qhd,kd->qhk",
                    query_block_rows,
                    key_block_rows,
                    preferred_element_type=jnp.float32,
                )
                * score_scale
            )
            allowed = (query_starts[:, None] == key_starts[None, :]) & (
                query_positions[:, None] >= key_positions[None, :]
            )
            scores = jnp.where(allowed[:, None, :], scores, MASKED)
            new_max = jnp.maximum(running_max, jnp.max(scores, axis=2))
            exponent = jnp.exp(scores - new_max[:, :, None])
            rescale = jnp.exp(running_max - new_max)
            running_sum = running_sum * rescale + jnp.sum(exponent, axis=2)
            running_out = running_out * rescale[:, :, None] + jnp.einsum(
                "qhk,kd->qhd",
                exponent.astype(jnp.bfloat16),
                value_block_rows,
                preferred_element_type=jnp.float32,
            )
            return (new_max, running_sum, running_out)

        lowest = 0
        initial = (
            jnp.full((TILE_ROWS, head_count), MASKED, jnp.float32),
            jnp.zeros((TILE_ROWS, head_count), jnp.float32),
            jnp.zeros((TILE_ROWS, head_count, stream_query.shape[2]), jnp.float32),
        )
        final_max, final_sum, final_out = lax.fori_loop(lowest, block_index + 1, add_block, initial)
        return (
            (final_out / final_sum[:, :, None])
            .reshape(TILE_ROWS, head_count * stream_query.shape[2])
            .astype(jnp.bfloat16)
        )

    outputs = lax.map(one_block, jnp.arange(stream_rows // TILE_ROWS, dtype=jnp.int32))
    return outputs.reshape(stream_rows, head_count * stream_query.shape[2])


def shards(queries, keys, values, doc_lengths, dest_group, dest_slot):
    group_total = lax.axis_size("rep")
    device_count = lax.axis_size("sp")
    tokens = queries.shape[0]
    capacity = 2 * DEVICE_PIECES // group_total
    group_self = lax.axis_index("rep")
    shard_self = lax.axis_index("sp")
    groups_all, order_rank = route_ranks(dest_group, group_total, device_count)
    slots_all = dest_slot.reshape(group_total, device_count, DEVICE_PIECES)
    sending = send_table(groups_all, order_rank, group_self, shard_self, group_total, capacity)
    receiving = receive_table(groups_all, order_rank, slots_all, group_self, capacity)
    lengths_self = doc_lengths[0]
    score_scale = 1.0 / math.sqrt(HEAD_WIDTH)
    head_count = QUERY_HEADS // device_count
    head_repeat_count = device_count // KEY_VALUE_HEADS
    query_pieces = queries.reshape(
        DEVICE_PIECES, PIECE_LENGTH, device_count, head_count * HEAD_WIDTH
    )
    key_piece_list = jnp.repeat(
        keys.reshape(DEVICE_PIECES, PIECE_LENGTH, KEY_VALUE_HEADS, HEAD_WIDTH),
        head_repeat_count,
        axis=2,
    )
    value_piece_list = jnp.repeat(
        values.reshape(DEVICE_PIECES, PIECE_LENGTH, KEY_VALUE_HEADS, HEAD_WIDTH),
        head_repeat_count,
        axis=2,
    )
    send_query = arrange(sending, query_pieces, "dcj,jpsf->dcpsf")
    send_key = arrange(sending, key_piece_list, "dcj,jpsf->dcpsf")
    send_value = arrange(sending, value_piece_list, "dcj,jpsf->dcpsf")
    got_query, got_key, got_value = (
        lax.all_to_all(
            lax.all_to_all(send_query, "rep", split_axis=0, concat_axis=0, tiled=True),
            "sp",
            split_axis=3,
            concat_axis=3,
            tiled=True,
        ),
        lax.all_to_all(
            lax.all_to_all(send_key, "rep", split_axis=0, concat_axis=0, tiled=True),
            "sp",
            split_axis=3,
            concat_axis=3,
            tiled=True,
        ),
        lax.all_to_all(
            lax.all_to_all(send_value, "rep", split_axis=0, concat_axis=0, tiled=True),
            "sp",
            split_axis=3,
            concat_axis=3,
            tiled=True,
        ),
    )
    form = "tzgc,gcptf->tzpf"
    stream_rows = device_count * tokens
    stream_query = arrange(receiving, got_query, form).reshape(stream_rows, head_count, HEAD_WIDTH)
    stream_key = arrange(receiving, got_key, form).reshape(stream_rows, HEAD_WIDTH)
    stream_value = arrange(receiving, got_value, form).reshape(stream_rows, HEAD_WIDTH)
    starts = doc_starts(jnp.arange(stream_rows, dtype=jnp.int32), lengths_self)
    attended = heads_attention(stream_query, stream_key, stream_value, starts, score_scale)
    return lax.all_to_all(attended, "sp", split_axis=0, concat_axis=1, tiled=True)


def solution(mesh):
    return jax.shard_map(
        shards,
        mesh=mesh,
        in_specs=(
            P(("rep", "sp"), None),
            P(("rep", "sp"), None),
            P(("rep", "sp"), None),
            P("rep", None),
            P(),
            P(),
        ),
        out_specs=P(("rep", "sp"), None),
        check_vma=False,
    )
```

profile of v0, /device:TPU:10, one launch (start us, length us, event | category | flops | bytes accessed | tf_op | source)
XLA Modules:
  0.0 629.0 jit_solution(14678788134078987252)
XLA Ops:
  3.6 1.5 copy.82
  5.1 3.5 all-to-all-start.2
  9.7 1.5 copy.86
  11.2 11.9 %all-to-all-done.2 = bf16[4,4,32,8,128]{4,1,2,3,0:T(4,128)(2,1)S(1)} async-done(((bf16[4,4,32,8,128]{4,1,2,3,0:T(4,128)(2,1)}), bf16[4,4,32,8,128]{4,1,2,3,0:T(4,128)(2,1)S(1)}, u32[]{:S(2)}, u32[]{:S(2)}) %all-to-all-start.2) | async-done | bytes 1048608 | tf_op jit(solution)/shard_map/all_to_all | solution.py:153
  23.1 3.5 all-to-all-start.4
  26.6 1.4 copy.83
  28.0 13.0 %all-to-all-done.4 = bf16[4,4,32,8,128]{4,1,2,3,0:T(4,128)(2,1)S(1)} async-done(((bf16[4,4,32,8,128]{4,1,2,3,0:T(4,128)(2,1)}), bf16[4,4,32,8,128]{4,1,2,3,0:T(4,128)(2,1)S(1)}, u32[]{:S(2)}, u32[]{:S(2)}) %all-to-all-start.4) | async-done | bytes 1048608 | tf_op jit(solution)/shard_map/all_to_all | solution.py:160
  41.0 6.2 all-to-all-start.3
  47.3 6.5 %copy.107 = bf16[32,8,8,1024]{3,2,1,0:T(8,128)(2,1)S(1)} copy(bf16[32,8,8,1024]{3,1,2,0:T(8,128)(2,1)} %bitcast.112) | data formatting | bytes 8388608
  53.8 2.5 bitcast_bitcast_fusion
  56.2 15.1 %convolution_convert_fusion = bf16[4,4,32,8,1024]{4,0,1,2,3:T(4,128)(2,1)} fusion(bf16[8,32,8,1024,1]{3,2,1,0,4:T(8,128)(2,1)} %bitcast_bitcast_fusion, pred[4,8]{1,0:T(4,128)(4,1)S(1)} %iota_compare_fusion.6, pred[4,8]{1,0:T(4,128)(4,1)S(1)} %iota_compare_fusion.7), kind=kOutput, calls=%fused_computation.27 | convolution fusion | flops 71303296 | bytes 12582976 | tf_op jit(solution)/shard_map/dcj,jpsf->dcpsf/dot_general | solution.py:49
  71.3 9.4 %copy.77 = bf16[4,4,32,8,1024]{4,1,2,3,0:T(4,128)(2,1)} copy(bf16[4,4,32,8,1024]{4,0,1,2,3:T(4,128)(2,1)} %convolution_convert_fusion) | data formatting | bytes 16777216 | tf_op jit(solution)/shard_map/convert_element_type | solution.py:49
  80.8 5.9 all-to-all-start
  86.7 1.4 copy.87
  88.0 91.8 %all-to-all-done = bf16[4,4,32,8,1024]{4,1,2,3,0:T(4,128)(2,1)} async-done(((bf16[4,4,32,8,1024]{4,1,2,3,0:T(4,128)(2,1)}), bf16[4,4,32,8,1024]{4,1,2,3,0:T(4,128)(2,1)}, u32[]{:S(2)}, u32[]{:S(2)}) %all-to-all-start) | async-done | bytes 8388640 | tf_op jit(solution)/shard_map/all_to_all | solution.py:146
  179.8 6.0 all-to-all-start.5
  185.8 8.6 %copy.78 = bf16[4,4,32,8,1024]{4,1,0,2,3:T(4,128)(2,1)} copy(bf16[4,4,32,8,1024]{4,1,2,3,0:T(4,128)(2,1)} %all-to-all-done) | data formatting | bytes 16777216 | tf_op jit(solution)/shard_map/all_to_all | solution.py:146
  194.4 13.7 %all-to-all-done.5 = bf16[4,4,32,8,128]{4,1,0,2,3:T(4,128)(2,1)S(1)} async-done(((bf16[4,4,32,8,128]{4,1,0,2,3:T(4,128)(2,1)}), bf16[4,4,32,8,128]{4,1,0,2,3:T(4,128)(2,1)S(1)}, u32[]{:S(2)}, u32[]{:S(2)}) %all-to-all-start.5) | async-done | bytes 1048608 | tf_op jit(solution)/shard_map/all_to_all | solution.py:159
  208.1 8.3 %all-to-all-start.1 = ((bf16[4,4,32,8,1024]{4,1,0,2,3:T(4,128)(2,1)}), bf16[4,4,32,8,1024]{4,1,0,2,3:T(4,128)(2,1)}, u32[]{:S(2)}, u32[]{:S(2)}) async-start(bf16[4,4,32,8,1024]{4,1,0,2,3:T(4,128)(2,1)} %copy.78), calls=%async_computation.1 | async-start | bytes 16777216 | tf_op jit(solution)/shard_map/all_to_all | solution.py:145
  220.5 174.5 %all-to-all-done.1 = bf16[4,4,32,8,1024]{4,1,0,2,3:T(4,128)(2,1)} async-done(((bf16[4,4,32,8,1024]{4,1,0,2,3:T(4,128)(2,1)}), bf16[4,4,32,8,1024]{4,1,0,2,3:T(4,128)(2,1)}, u32[]{:S(2)}, u32[]{:S(2)}) %all-to-all-start.1) | async-done | bytes 8388640 | tf_op jit(solution)/shard_map/all_to_all | solution.py:145
  395.0 7.6 %bitcast_convert_fusion = bf16[8,8,32,1024]{3,1,2,0:T(8,128)(2,1)S(1)} fusion(bf16[8,8,4,4,1]{1,3,2,4,0:T(4,128)(2,1)S(1)} %fusion.22, bf16[4,4,32,8,1024]{4,1,0,2,3:T(4,128)(2,1)} %all-to-all-done.1), kind=kOutput, calls=%fused_computation.26 | convolution fusion | flops 69206016 | bytes 12584960 | tf_op jit(solution)/shard_map/tzgc,gcptf->tzpf/dot_general | solution.py:49
  402.6 2.5 copy.79
  405.0 3.0 copy.108
  408.1 109.6 %while.26 = (s32[]{:T(128)}, bf16[4,512,1024]{2,1,0:T(8,128)(2,1)}, s32[4]{0:T(128)S(1)}, bf16[2048,8,128]{2,1,0:T(8,128)(2,1)}, s32[2048]{0:T(1024)S(1)}, /*ind...) while((s32[]{:T(128)}, bf16[4,512,1024]{2,1,0:T(8,128)(2,1)}, ...), condition=%wide.region_8.9_spmd, body=%wide.region_3.8_spmd.sunk | while | flops 1099703296 | bytes 47780944 | solution.py:109
  409.4 1.3 constant_dynamic-slice_fusion.2
  411.6 8.4 %while.27 = (s32[]{:T(128)}, f32[512,8]{0,1:T(8,128)S(1)}, f32[512,8]{0,1:T(8,128)S(1)}, f32[512,8,128]{2,0,1:T(8,128)S(1)}, s32[]{:T(128)}, /*index=5*/s32[512]...) while((s32[]{:T(128)}, f32[512,8]{0,1:T(8,128)S(1)}, ...), condition=%wide.region_7.7_spmd.clone, body=%wide.region_4.6_spmd.clone.sunk | while | flops 1098654720 | bytes 31998160 | solution.py:102
  412.0 2.4 fusion.58
  414.4 1.7 fusion.59
  416.2 3.8 multiply_add_fusion.5
  424.2 1.3 constant_dynamic-slice_fusion.2
  426.5 16.7 %while.27 = (s32[]{:T(128)}, f32[512,8]{0,1:T(8,128)S(1)}, f32[512,8]{0,1:T(8,128)S(1)}, f32[512,8,128]{2,0,1:T(8,128)S(1)}, s32[]{:T(128)}, /*index=5*/s32[512]...) while((s32[]{:T(128)}, f32[512,8]{0,1:T(8,128)S(1)}, ...), condition=%wide.region_7.7_spmd.clone, body=%wide.region_4.6_spmd.clone.sunk | while | flops 1098654720 | bytes 31998160 | solution.py:102
  426.9 2.4 fusion.58
  429.3 1.7 fusion.59
  431.1 3.8 multiply_add_fusion.5
  435.2 2.4 fusion.58
  437.6 1.7 fusion.59
  439.4 3.8 multiply_add_fusion.5
  449.7 25.1 %while.27 = (s32[]{:T(128)}, f32[512,8]{0,1:T(8,128)S(1)}, f32[512,8]{0,1:T(8,128)S(1)}, f32[512,8,128]{2,0,1:T(8,128)S(1)}, s32[]{:T(128)}, /*index=5*/s32[512]...) while((s32[]{:T(128)}, f32[512,8]{0,1:T(8,128)S(1)}, ...), condition=%wide.region_7.7_spmd.clone, body=%wide.region_4.6_spmd.clone.sunk | while | flops 1098654720 | bytes 31998160 | solution.py:102
  450.1 2.4 fusion.58
  452.5 1.7 fusion.59
  454.3 3.8 multiply_add_fusion.5
  458.4 2.4 fusion.58
  460.9 1.7 fusion.59
  462.6 3.8 multiply_add_fusion.5
  466.8 2.4 fusion.58
  469.2 1.7 fusion.59
  471.0 3.8 multiply_add_fusion.5
  479.1 1.3 constant_dynamic-slice_fusion.2
  481.3 33.5 %while.27 = (s32[]{:T(128)}, f32[512,8]{0,1:T(8,128)S(1)}, f32[512,8]{0,1:T(8,128)S(1)}, f32[512,8,128]{2,0,1:T(8,128)S(1)}, s32[]{:T(128)}, /*index=5*/s32[512]...) while((s32[]{:T(128)}, f32[512,8]{0,1:T(8,128)S(1)}, ...), condition=%wide.region_7.7_spmd.clone, body=%wide.region_4.6_spmd.clone.sunk | while | flops 1098654720 | bytes 31998160 | solution.py:102
  481.7 2.4 fusion.58
  484.1 1.7 fusion.59
  485.9 3.8 multiply_add_fusion.5
  490.0 2.4 fusion.58
  492.5 1.7 fusion.59
  494.2 3.8 multiply_add_fusion.5
  498.4 2.4 fusion.58
  500.8 1.7 fusion.59
  502.6 3.8 multiply_add_fusion.5
  506.8 2.4 fusion.58
  509.2 1.7 fusion.59
  511.0 3.8 multiply_add_fusion.5
  517.7 98.5 %all_to_all.49 = bf16[8,256,1024]{2,1,0:T(8,128)(2,1)} all-to-all(bf16[8,256,1024]{2,1,0:T(8,128)(2,1)} %bitcast.113), channel_id=1, replica_groups=mesh['rep'=4,'sp'=8] {'sp'}, dimensions={0} | all-to-all | bytes 8388608 | tf_op jit(solution)/shard_map/all_to_all | solution.py:174
  616.2 6.5 %copy.90 = bf16[8,256,1024]{1,2,0:T(8,128)(2,1)} copy(bf16[8,256,1024]{2,1,0:T(8,128)(2,1)} %all_to_all.49) | data formatting | bytes 8388608 | tf_op jit(solution)/shard_map/all_to_all | solution.py:174
  622.7 6.3 %copy.91 = bf16[256,8192]{1,0:T(8,128)(2,1)} copy(bf16[256,8192]{0,1:T(8,128)(2,1)} %bitcast.110) | data formatting | bytes 8388608 | tf_op jit(solution)/shard_map/all_to_all | solution.py:174
  (136 shorter events, 29.2 us)
Async XLA Ops:
  0.0 8.7 %copy-start = (bf16[256,1024]{1,0:T(8,128)(2,1)S(1)}, bf16[256,1024]{1,0:T(8,128)(2,1)}, u32[]{:S(2)}) copy-start(bf16[256,1024]{1,0:T(8,128)(2,1)} %param.12) | copy-start | bytes 1572868
  5.1 18.0 %all-to-all-start.2 = ((bf16[4,4,32,8,128]{4,1,2,3,0:T(4,128)(2,1)}), bf16[4,4,32,8,128]{4,1,2,3,0:T(4,128)(2,1)S(1)}, u32[]{:S(2)}, u32[]{:S(2)}) async-start(bf16[4,4,32,8,128]{4,1,2,3,0:T(4,128)(2,1)} %copy.82), calls=%async_computation.2 | async-start | bytes 2097152 | tf_op jit(solution)/shard_map/all_to_all | solution.py:153
  23.1 18.0 %all-to-all-start.4 = ((bf16[4,4,32,8,128]{4,1,2,3,0:T(4,128)(2,1)}), bf16[4,4,32,8,128]{4,1,2,3,0:T(4,128)(2,1)S(1)}, u32[]{:S(2)}, u32[]{:S(2)}) async-start(bf16[4,4,32,8,128]{4,1,2,3,0:T(4,128)(2,1)} %copy.86), calls=%async_computation.4 | async-start | bytes 2097152 | tf_op jit(solution)/shard_map/all_to_all | solution.py:160
  41.0 39.8 %all-to-all-start.3 = ((bf16[4,4,32,8,128]{4,1,0,2,3:T(4,128)(2,1)}), bf16[4,4,32,8,128]{4,1,0,2,3:T(4,128)(2,1)S(1)}, u32[]{:S(2)}, u32[]{:S(2)}) async-start(bf16[4,4,32,8,128]{4,1,0,2,3:T(4,128)(2,1)} %copy.83), calls=%async_computation.3 | async-start | bytes 2097152 | tf_op jit(solution)/shard_map/all_to_all | solution.py:152
  80.8 99.1 %all-to-all-start = ((bf16[4,4,32,8,1024]{4,1,2,3,0:T(4,128)(2,1)}), bf16[4,4,32,8,1024]{4,1,2,3,0:T(4,128)(2,1)}, u32[]{:S(2)}, u32[]{:S(2)}) async-start(bf16[4,4,32,8,1024]{4,1,2,3,0:T(4,128)(2,1)} %copy.77), calls=%async_computation | async-start | bytes 16777216 | tf_op jit(solution)/shard_map/all_to_all | solution.py:146
  179.8 28.3 %all-to-all-start.5 = ((bf16[4,4,32,8,128]{4,1,0,2,3:T(4,128)(2,1)}), bf16[4,4,32,8,128]{4,1,0,2,3:T(4,128)(2,1)S(1)}, u32[]{:S(2)}, u32[]{:S(2)}) async-start(bf16[4,4,32,8,128]{4,1,0,2,3:T(4,128)(2,1)} %copy.87), calls=%async_computation.5 | async-start | bytes 2097152 | tf_op jit(solution)/shard_map/all_to_all | solution.py:159
  194.4 22.1 %copy-start.1 = (s32[4,64]{1,0:T(4,128)S(1)}, s32[4,64]{1,0:T(4,128)}, u32[]{:S(2)}) copy-start(s32[4,64]{1,0:T(4,128)} %param.15) | copy-start | bytes 3076
  194.4 22.2 %copy-start.2 = (s32[1,16]{1,0:T(1,128)S(1)}, s32[1,16]{1,0:T(1,128)}, u32[]{:S(2)}) copy-start(s32[1,16]{1,0:T(1,128)} %param.13) | copy-start | bytes 196
  208.1 186.9 %all-to-all-start.1 = ((bf16[4,4,32,8,1024]{4,1,0,2,3:T(4,128)(2,1)}), bf16[4,4,32,8,1024]{4,1,0,2,3:T(4,128)(2,1)}, u32[]{:S(2)}, u32[]{:S(2)}) async-start(bf16[4,4,32,8,1024]{4,1,0,2,3:T(4,128)(2,1)} %copy.78), calls=%async_computation.1 | async-start | bytes 16777216 | tf_op jit(solution)/shard_map/all_to_all | solution.py:145
where the time goes:
time: 634 us; the launch traced here: 629 us
  waiting for transfers between devices  305 us (48%)
  blocking collectives  98.5 us (16%)
  matrix products  87.8 us (14%)
  local copies, waits for them, and re-layouts  73.8 us (12%)
  starting transfers between devices  33.5 us (5%)
  other arithmetic  24.3 us (4%)
    all_to_all x1, waiting for transfers between devices, shards(): lax.all_to_all(lax.all_to_all(send_query, 'rep', split_axis=0, concat_axi...  174 us
    all_to_all x1, blocking collectives, shards(): lax.all_to_all(attended, 'sp', split_axis=0, concat_axis=1, tiled=True)  98.5 us
    all_to_all x1, waiting for transfers between devices, shards(): lax.all_to_all(send_query, 'rep', split_axis=0, concat_axis=0, tiled=True)  91.8 us
    dot_general x10, matrix products, add_block(): jnp.einsum('qhk,kd->qhd', exponent.astype(jnp.bfloat16), value_block_rows...  37.6 us
    dot_general x6, matrix products, arrange(): jnp.einsum(form, table, arrived_rows, preferred_element_type=jnp.float32)  25.9 us
    dot_general x10, matrix products, add_block(): jnp.einsum('qhd,kd->qhk', query_block_rows, key_block_rows, preferred_ele...  24 us
    reduce_sum x10, other arithmetic, add_block(): running_sum = running_sum * rescale + jnp.sum(exponent, axis=2)  17.4 us
    convert_element_type x6, local copies, waits for them, and re-layouts, arrange(): jnp.einsum(form, table, arrived_rows, preferred_element_type=jnp.float32)  16.8 us
  transfers between devices with their start and end apart: 6, of which 5 were waited for; matrix products, arithmetic and copies ran while one was open for 8% of the time, Pallas kernels for 0%

commit v1 on v0

v1 whole, which is shorter than its diff:
```python
import functools
import math

import jax
import jax.numpy as jnp
from jax import lax
from jax.experimental import pallas as pl
from jax.experimental.pallas import tpu as pltpu
from jax.sharding import PartitionSpec as P

QUERY_HEADS = 64
KEY_VALUE_HEADS = 8
HEAD_WIDTH = 128
DEVICE_PIECES = 8
PIECE_LENGTH = 32
HEADS_PER_KV = QUERY_HEADS // KEY_VALUE_HEADS
CHUNK = HEADS_PER_KV * HEAD_WIDTH
CHUNKS = KEY_VALUE_HEADS
BLOCK = DEVICE_PIECES * PIECE_LENGTH
HALF_PIECES = 4
HALF_ROWS = HALF_PIECES * PIECE_LENGTH
DEPTH = 3

MASKED = -1e30
MESH = pl.DeviceIdType.MESH


def kernel(
    groups,
    shard_count,
    halo,
    lengths_ref,
    group_ref,
    slot_ref,
    q_hbm,
    k_hbm,
    v_hbm,
    o_hbm,
    *scratch,
):
    qbufs = scratch[:CHUNKS]
    (
        kbuf,
        vbuf,
        kp,
        vp,
        bias,
        qsel,
        obuf,
        sel,
        local_sem,
        y_send,
        y_recv,
        m_send,
        m_recv,
        f_send,
        f_recv,
        halo_send,
        halo_recv,
        out_sem,
    ) = scratch[CHUNKS:]
    rep = lax.axis_index("rep")
    shard = lax.axis_index("sp")
    chips = groups // 2
    core = lax.rem(rep, 2)
    chip = lax.div(rep, 2)
    mate = chip * 2 + (1 - core)
    window = halo * BLOCK + HALF_ROWS
    own_first = halo * BLOCK

    def peer(step):
        return lax.rem(chip + step, chips) * 2 + core

    def source(step):
        return lax.rem(chip + chips - step, chips) * 2 + core

    def mate_source(step):
        return lax.rem(chip + chips - step, chips) * 2 + (1 - core)

    items = CHUNKS + 2

    def original(item):
        if item == 0:
            return k_hbm
        if item == 1:
            return v_hbm
        return q_hbm.at[:, :, pl.ds((item - 2) * CHUNK, CHUNK)]

    def landing(item, group):
        buffer = (kbuf, vbuf, *qbufs)[item]
        return buffer.at[pl.ds(group * DEVICE_PIECES, DEVICE_PIECES)]

    def local_copy(item):
        return pltpu.make_async_copy(original(item), landing(item, rep), local_sem.at[item])

    def mate_copy(item, group):
        return pltpu.make_async_remote_copy(
            src_ref=original(item),
            dst_ref=landing(item, group),
            send_sem=m_send.at[item],
            recv_sem=m_recv.at[item],
            device_id={"rep": mate},
            device_id_type=MESH,
        )

    def peer_copy(item, step, group):
        return pltpu.make_async_remote_copy(
            src_ref=original(item),
            dst_ref=landing(item, group),
            send_sem=y_send.at[item, step - 1],
            recv_sem=y_recv.at[item, step - 1],
            device_id={"rep": peer(step)},
            device_id_type=MESH,
        )

    def forward_copy(item, step, group):
        return pltpu.make_async_remote_copy(
            src_ref=landing(item, group),
            dst_ref=landing(item, group),
            send_sem=f_send.at[item, step - 1],
            recv_sem=f_recv.at[item, step - 1],
            device_id={"rep": mate},
            device_id_type=MESH,
        )

    def start_out(item):
        for step in range(1, chips):
            peer_copy(item, step, rep).start()

    def start_near(item):
        mate_copy(item, rep).start()
        local_copy(item).start()

    def pass_on(item):
        for step in range(1, chips):
            peer_copy(item, step, source(step)).wait_recv()
            forward_copy(item, step, source(step)).start()

    def all_here(item):
        local_copy(item).wait()
        mate_copy(item, mate).wait_recv()
        for step in range(1, chips):
            forward_copy(item, step, mate_source(step)).wait_recv()

    def halo_copy(which, distance):
        placed = (kp, vp)[which]
        return pltpu.make_async_remote_copy(
            src_ref=placed.at[:, pl.ds(own_first, BLOCK), :],
            dst_ref=placed.at[:, pl.ds((halo - distance) * BLOCK, BLOCK), :],
            send_sem=halo_send.at[which, distance - 1],
            recv_sem=halo_recv.at[which, distance - 1],
            device_id={"sp": lax.rem(shard + distance, shard_count)},
            device_id_type=MESH,
        )

    barrier = pltpu.get_barrier_semaphore()
    pl.semaphore_signal(barrier, inc=1, device_id={"rep": mate}, device_id_type=MESH)
    for step in range(1, chips):
        pl.semaphore_signal(barrier, inc=1, device_id={"rep": peer(step)}, device_id_type=MESH)
    for distance in range(1, halo + 1):

        @pl.when(shard + distance < shard_count)
        def _():
            pl.semaphore_signal(
                barrier, inc=1, device_id={"sp": shard + distance}, device_id_type=MESH
            )

        @pl.when(shard >= distance)
        def _():
            pl.semaphore_signal(
                barrier, inc=1, device_id={"sp": shard - distance}, device_id_type=MESH
            )

    before = jnp.minimum(shard, halo)
    after = jnp.minimum(shard_count - 1 - shard, halo)
    pl.semaphore_wait(barrier, chips + before + after)

    for item in range(2):
        start_out(item)
    for item in range(2):
        start_near(item)
    for item in range(2, 2 + DEPTH):
        start_out(item)
        start_near(item)

    def find_slot(slot, carry):
        found = jnp.int32(0)
        for group in range(groups):
            for piece in range(DEVICE_PIECES):
                column = shard * DEVICE_PIECES + piece
                hit = (group_ref[group, column] == rep) & (slot_ref[group, column] == slot)
                found = jnp.where(hit, group * DEVICE_PIECES + piece, found)
        sel[slot] = found
        return carry

    lax.fori_loop(0, DEVICE_PIECES, find_slot, 0)

    def first_token(positions):
        end = jnp.int32(0)
        first = jnp.zeros_like(positions)
        for document in range(lengths_ref.shape[1]):
            length = lengths_ref[0, document]
            end = end + length
            first = first + jnp.where(positions >= end, length, 0)
        return first

    for half in range(2):
        key_begin = (shard - halo) * BLOCK + half * HALF_ROWS
        key_positions = key_begin + lax.broadcasted_iota(jnp.int32, (1, window), 1)
        key_first = jnp.where(key_positions >= 0, first_token(key_positions), -1)
        query_begin = shard * BLOCK + half * HALF_ROWS
        query_positions = query_begin + lax.broadcasted_iota(jnp.int32, (HALF_ROWS, 1), 0)
        query_first = first_token(query_positions)
        allowed = (query_first == key_first) & (query_positions >= key_positions)
        bias[pl.ds(half * HALF_ROWS, HALF_ROWS), :] = jnp.where(allowed, 0.0, MASKED)

    for distance in range(1, halo + 1):

        @pl.when(shard < distance)
        def _():
            empty = jnp.zeros((KEY_VALUE_HEADS, BLOCK, HEAD_WIDTH), jnp.bfloat16)
            kp[:, pl.ds((halo - distance) * BLOCK, BLOCK), :] = empty
            vp[:, pl.ds((halo - distance) * BLOCK, BLOCK), :] = empty

    for item in range(2):
        pass_on(item)
    for item in range(2):
        all_here(item)
        arrived, placed = (kbuf, vbuf)[item], (kp, vp)[item]
        for slot in range(DEVICE_PIECES):
            piece = arrived[sel[slot]]
            for head in range(KEY_VALUE_HEADS):
                placed[head, pl.ds(own_first + slot * PIECE_LENGTH, PIECE_LENGTH), :] = piece[
                    :, head * HEAD_WIDTH : (head + 1) * HEAD_WIDTH
                ]
        for distance in range(1, halo + 1):

            @pl.when(shard + distance < shard_count)
            def _():
                halo_copy(item, distance).start()

    factor = math.log2(math.e) / math.sqrt(HEAD_WIDTH)

    def out_copy(head):
        return pltpu.make_async_copy(
            obuf.at[lax.rem(head, 2)],
            o_hbm.at[:, pl.ds(pl.multiple_of(head * CHUNK, CHUNK), CHUNK)],
            out_sem.at[lax.rem(head, 2)],
        )

    def attend(head):
        buffer = lax.rem(head, 2)

        def one_piece(slot, carry):
            half = lax.div(slot, HALF_PIECES)
            keys_at = pl.ds(pl.multiple_of(half * HALF_ROWS, HALF_ROWS), window)
            rows_at = pl.ds(pl.multiple_of(slot * PIECE_LENGTH, PIECE_LENGTH), PIECE_LENGTH)
            piece = qsel[slot]
            query = jnp.concatenate(
                [piece[:, i * HEAD_WIDTH : (i + 1) * HEAD_WIDTH] for i in range(HEADS_PER_KV)],
                axis=0,
            )
            scores = lax.dot_general(
                query,
                kp[head, keys_at, :],
                (((1,), (1,)), ((), ())),
                preferred_element_type=jnp.float32,
            )
            scores = scores.reshape(HEADS_PER_KV, PIECE_LENGTH, window) * factor
            scores = (scores + bias[rows_at, :][None]).reshape(BLOCK, window)
            peak = jnp.max(scores, axis=1, keepdims=True)
            exponent = jnp.exp2(scores - peak)
            total = jnp.sum(exponent, axis=1, keepdims=True)
            summed = jnp.dot(
                exponent.astype(jnp.bfloat16),
                vp[head, keys_at, :],
                preferred_element_type=jnp.float32,
            )
            result = (summed / total).astype(jnp.bfloat16)
            for i in range(HEADS_PER_KV):
                obuf[buffer, rows_at, i * HEAD_WIDTH : (i + 1) * HEAD_WIDTH] = result[
                    i * PIECE_LENGTH : (i + 1) * PIECE_LENGTH
                ]
            return carry

        lax.fori_loop(0, DEVICE_PIECES, one_piece, 0)

    def turn(count, carry):
        for chunk in range(CHUNKS):

            @pl.when(count == chunk)
            def _():
                pass_on(2 + chunk)
                if chunk + DEPTH < CHUNKS:
                    for step in range(1, chips):
                        peer_copy(2 + chunk, step, rep).wait_send()
                    start_out(2 + chunk + DEPTH)
                    start_near(2 + chunk + DEPTH)

        @pl.when(count == 1)
        def _():
            for distance in range(1, halo + 1):

                @pl.when(shard >= distance)
                def _():
                    for which in range(2):
                        halo_copy(which, distance).wait_recv()

        for chunk in range(CHUNKS):

            @pl.when(count == chunk + 1)
            def _():
                all_here(2 + chunk)
                for slot in range(DEVICE_PIECES):
                    qsel[slot] = qbufs[chunk][sel[slot]]

        @pl.when(count >= 1)
        def _():
            head = count - 1

            @pl.when(count >= 3)
            def _():
                out_copy(head - 2).wait()

            attend(head)
            out_copy(head).start()

        return carry

    lax.fori_loop(0, CHUNKS + 1, turn, 0)

    for head in range(CHUNKS - 2, CHUNKS):
        out_copy(head).wait()
    for item in range(items):
        mate_copy(item, rep).wait_send()
        for step in range(1, chips):
            if item < 2 or item - 2 + DEPTH >= CHUNKS:
                peer_copy(item, step, rep).wait_send()
            forward_copy(item, step, source(step)).wait_send()
    for distance in range(1, halo + 1):

        @pl.when(shard + distance < shard_count)
        def _():
            for which in range(2):
                halo_copy(which, distance).wait_send()


def shards(queries, keys, values, doc_lengths, dest_group, dest_slot):
    groups = lax.axis_size("rep")
    shard_count = lax.axis_size("sp")
    chips = groups // 2
    halo = shard_count // 4
    pieces = groups * DEVICE_PIECES
    items = CHUNKS + 2
    key_rows = (halo + 1) * BLOCK
    window = halo * BLOCK + HALF_ROWS
    wide = KEY_VALUE_HEADS * HEAD_WIDTH
    smem = pl.BlockSpec(memory_space=pltpu.SMEM)
    hbm = pl.BlockSpec(memory_space=pl.ANY)
    dma = pltpu.SemaphoreType.DMA
    scratch = [pltpu.VMEM((pieces, PIECE_LENGTH, CHUNK), jnp.bfloat16) for _ in range(CHUNKS)]
    scratch += [
        pltpu.VMEM((pieces, PIECE_LENGTH, wide), jnp.bfloat16),
        pltpu.VMEM((pieces, PIECE_LENGTH, wide), jnp.bfloat16),
        pltpu.VMEM((KEY_VALUE_HEADS, key_rows, HEAD_WIDTH), jnp.bfloat16),
        pltpu.VMEM((KEY_VALUE_HEADS, key_rows, HEAD_WIDTH), jnp.bfloat16),
        pltpu.VMEM((BLOCK, window), jnp.float32),
        pltpu.VMEM((DEVICE_PIECES, PIECE_LENGTH, CHUNK), jnp.bfloat16),
        pltpu.VMEM((2, BLOCK, CHUNK), jnp.bfloat16),
        pltpu.SMEM((DEVICE_PIECES,), jnp.int32),
        dma((items,)),
        dma((items, chips - 1)),
        dma((items, chips - 1)),
        dma((items,)),
        dma((items,)),
        dma((items, chips - 1)),
        dma((items, chips - 1)),
        dma((2, halo)),
        dma((2, halo)),
        dma((2,)),
    ]
    work = QUERY_HEADS * BLOCK * window
    return pl.pallas_call(
        functools.partial(kernel, groups, shard_count, halo),
        out_shape=jax.ShapeDtypeStruct(queries.shape, jnp.bfloat16),
        in_specs=[smem, smem, smem, hbm, hbm, hbm],
        out_specs=hbm,
        scratch_shapes=scratch,
        cost_estimate=pl.CostEstimate(
            flops=4 * work * HEAD_WIDTH,
            bytes_accessed=4 * queries.size + 4 * keys.size,
            transcendentals=work,
        ),
        compiler_params=pltpu.CompilerParams(
            collective_id=0, has_side_effects=True, vmem_limit_bytes=56 * 1024 * 1024
        ),
    )(
        doc_lengths,
        dest_group,
        dest_slot,
        queries.reshape(DEVICE_PIECES, PIECE_LENGTH, QUERY_HEADS * HEAD_WIDTH),
        keys.reshape(DEVICE_PIECES, PIECE_LENGTH, wide),
        values.reshape(DEVICE_PIECES, PIECE_LENGTH, wide),
    )


def solution(mesh):
    return jax.shard_map(
        shards,
        mesh=mesh,
        in_specs=(
            P(("rep", "sp"), None),
            P(("rep", "sp"), None),
            P(("rep", "sp"), None),
            P("rep", None),
            P(),
            P(),
        ),
        out_specs=P(("rep", "sp"), None),
        check_vma=False,
    )
```

time: 634 us -> 134 us (0.21)
  waiting for transfers between devices: 305 us -> 0 us
  Pallas kernels: 0 us -> 128 us
  blocking collectives: 98.5 us -> 0 us
  matrix products: 87.8 us -> 0 us
  local copies, waits for them, and re-layouts: 73.8 us -> 4.64 us
  starting transfers between devices: 33.5 us -> 0 us
  other arithmetic: 24.3 us -> 0 us
    all_to_all x6 -> x0, waiting for transfers between devices: 305 us -> none  [the longest x1 174 us: shards(): lax.all_to_all(lax.all_to_all(send_query, 'rep', split_axis=0, concat_axi...]
    pallas_call x0 -> x1, Pallas kernels: none -> 128 us  [shards(): pl.pallas_call(functools.partial(kernel, groups, shard_count, halo), out_...]
    all_to_all x1 -> x0, blocking collectives: 98.5 us -> none  [shards(): lax.all_to_all(attended, 'sp', split_axis=0, concat_axis=1, tiled=True)]
    dot_general x27 -> x0, matrix products: 87.8 us -> none  [the longest x10 37.6 us: add_block(): jnp.einsum('qhk,kd->qhd', exponent.astype(jnp.bfloat16), value_block_rows...]
    all_to_all x6 -> x0, starting transfers between devices: 33.5 us -> none  [the longest x1 8.33 us: shards(): lax.all_to_all(lax.all_to_all(send_query, 'rep', split_axis=0, concat_axi...]
    all_to_all x5 -> x0, local copies, waits for them, and re-layouts: 24.1 us -> none  [the longest x2 12.8 us: shards(): lax.all_to_all(attended, 'sp', split_axis=0, concat_axis=1, tiled=True)]
    convert_element_type x14 -> x0, local copies, waits for them, and re-layouts: 21.4 us -> none  [the longest x6 16.8 us: arrange(): jnp.einsum(form, table, arrived_rows, preferred_element_type=jnp.float32)]
    reduce_sum x12 -> x0, other arithmetic: 18.2 us -> none  [the longest x10 17.4 us: add_block(): running_sum = running_sum * rescale + jnp.sum(exponent, axis=2)]
  transfers between devices with their start and end apart: 6 -> 0, of which waited for: 5 -> 0; matrix products, arithmetic and copies ran while one was open for 8% -> 0% of each run, Pallas kernels for 0% -> 0%
where the time goes in v1:
time: 134 us; the launch traced here: 133 us
  Pallas kernels  128 us (96%)
  local copies, waits for them, and re-layouts  4.64 us (3%)
    pallas_call x1, Pallas kernels, shards(): pl.pallas_call(functools.partial(kernel, groups, shard_count, halo), out_...  128 us
    unnamed x1, local copies, waits for them, and re-layouts  4.64 us

profile of v1, /device:TPU:10, one launch (start us, length us, event | category | flops | bytes accessed | tf_op | source)
XLA Modules:
  0.0 132.7 jit_solution(17746170159538210699)
XLA Ops:
  0.0 128.0 %shard_map.64 = bf16[256,8192]{1,0:T(8,128)(2,1)} custom-call(s32[1,16]{1,0:T(1,128)} %lengths_ref.1, s32[4,64]{1,0:T(4,128)} %group_ref.1, s32[4,64]{1,0:T(4,128)} %slot_ref.1, bf16[8,32,8192]{2,1,0:T(8,128)(2,1)} %bitcast.3, bf16[8,32,1024]{2,1,0:T(8,128)(2,1)} %bitcast.4, bf16[8,32,1024]{2,1,0:T(8,128)(2,1)} %bitcast.5), custom_call_target="tpu_custom_call" | custom-call | flops 5368709120 | bytes 9437184 | tf_op jit(solution)/shard_map/pallas_call | solution.py:383
  128.0 4.6 %copy.8 = bf16[256,8192]{1,0:T(8,128)(2,1)} copy(bf16[256,8192]{1,0:T(8,128)(2,1)} %shard_map.64) | data formatting | bytes 8388608

commit v2 on v1

--- a/solution.py
+++ b/solution.py
@@ -19,6 +19,7 @@
 BLOCK = DEVICE_PIECES * PIECE_LENGTH
 HALF_PIECES = 4
 HALF_ROWS = HALF_PIECES * PIECE_LENGTH
+CAPACITY = 6
 DEPTH = 3
 
 MASKED = -1e30
@@ -29,6 +30,7 @@
     groups,
     shard_count,
     halo,
+    slim,
     lengths_ref,
     group_ref,
     slot_ref,
@@ -38,16 +40,20 @@
     o_hbm,
     *scratch,
 ):
-    qbufs = scratch[:CHUNKS]
+    items = CHUNKS + 2
+    buffers = scratch[:items]
+    far = scratch[items : 2 * items]
+    stage = scratch[2 * items : 3 * items]
     (
-        kbuf,
-        vbuf,
         kp,
         vp,
         bias,
         qsel,
         obuf,
         sel,
+        far_sel,
+        from_far,
+        send_sel,
         local_sem,
         y_send,
         y_recv,
@@ -58,7 +64,7 @@
         halo_send,
         halo_recv,
         out_sem,
-    ) = scratch[CHUNKS:]
+    ) = scratch[3 * items if slim else items :]
     rep = lax.axis_index("rep")
     shard = lax.axis_index("sp")
     chips = groups // 2
@@ -77,7 +83,6 @@
     def mate_source(step):
         return lax.rem(chip + chips - step, chips) * 2 + (1 - core)
 
-    items = CHUNKS + 2
 
     def original(item):
         if item == 0:
@@ -87,8 +92,13 @@
         return q_hbm.at[:, :, pl.ds((item - 2) * CHUNK, CHUNK)]
 
     def landing(item, group):
-        buffer = (kbuf, vbuf, *qbufs)[item]
-        return buffer.at[pl.ds(group * DEVICE_PIECES, DEVICE_PIECES)]
+        place = lax.rem(group, 2) if slim else group
+        return buffers[item].at[pl.ds(place * DEVICE_PIECES, DEVICE_PIECES)]
+
+    def crossing(item, group):
+        if slim:
+            return far[item].at[pl.ds(lax.rem(group, 2) * CAPACITY, CAPACITY)]
+        return landing(item, group)
 
     def local_copy(item):
         return pltpu.make_async_copy(original(item), landing(item, rep), local_sem.at[item])
@@ -105,8 +115,8 @@
 
     def peer_copy(item, step, group):
         return pltpu.make_async_remote_copy(
-            src_ref=original(item),
-            dst_ref=landing(item, group),
+            src_ref=stage[item] if slim else original(item),
+            dst_ref=crossing(item, group),
             send_sem=y_send.at[item, step - 1],
             recv_sem=y_recv.at[item, step - 1],
             device_id={"rep": peer(step)},
@@ -115,15 +125,23 @@
 
     def forward_copy(item, step, group):
         return pltpu.make_async_remote_copy(
-            src_ref=landing(item, group),
-            dst_ref=landing(item, group),
+            src_ref=crossing(item, group),
+            dst_ref=crossing(item, group),
             send_sem=f_send.at[item, step - 1],
             recv_sem=f_recv.at[item, step - 1],
             device_id={"rep": mate},
             device_id_type=MESH,
         )
 
+    def near_here(item):
+        local_copy(item).wait()
+        mate_copy(item, mate).wait_recv()
+
     def start_out(item):
+        if slim:
+            near_here(item)
+            for place in range(CAPACITY):
+                stage[item][place] = buffers[item][send_sel[place]]
         for step in range(1, chips):
             peer_copy(item, step, rep).start()
 
@@ -137,10 +155,16 @@
             forward_copy(item, step, source(step)).start()
 
     def all_here(item):
-        local_copy(item).wait()
-        mate_copy(item, mate).wait_recv()
+        if not slim:
+            near_here(item)
         for step in range(1, chips):
             forward_copy(item, step, mate_source(step)).wait_recv()
+
+    def pick(item, slot):
+        piece = buffers[item][sel[slot]]
+        if slim:
+            piece = jnp.where(from_far[slot] == 1, far[item][far_sel[slot]], piece)
+        return piece
 
     def halo_copy(which, distance):
         placed = (kp, vp)[which]
@@ -175,24 +199,59 @@
     after = jnp.minimum(shard_count - 1 - shard, halo)
     pl.semaphore_wait(barrier, chips + before + after)
 
-    for item in range(2):
-        start_out(item)
-    for item in range(2):
-        start_near(item)
-    for item in range(2, 2 + DEPTH):
-        start_out(item)
-        start_near(item)
+    if slim:
+        for item in range(2):
+            start_near(item)
+    else:
+        for item in range(2):
+            start_out(item)
+        for item in range(2):
+            start_near(item)
+        for item in range(2, 2 + DEPTH):
+            start_out(item)
+            start_near(item)
+
+    def table_at(of_chip, number):
+        group = of_chip * 2 + number // DEVICE_PIECES
+        return group, shard * DEVICE_PIECES + number % DEVICE_PIECES
 
     def find_slot(slot, carry):
         found = jnp.int32(0)
-        for group in range(groups):
-            for piece in range(DEVICE_PIECES):
-                column = shard * DEVICE_PIECES + piece
-                hit = (group_ref[group, column] == rep) & (slot_ref[group, column] == slot)
-                found = jnp.where(hit, group * DEVICE_PIECES + piece, found)
+        for number in range((2 if slim else groups) * DEVICE_PIECES):
+            at = table_at(chip if slim else 0, number)
+            hit = (group_ref[at] == rep) & (slot_ref[at] == slot)
+            found = jnp.where(hit, number, found)
         sel[slot] = found
+        if slim:
+            far_found, is_far, rank = jnp.int32(0), jnp.int32(0), jnp.int32(0)
+            for number in range(2 * DEVICE_PIECES):
+                at = table_at(1 - chip, number)
+                group = group_ref[at]
+                hit = (group == rep) & (slot_ref[at] == slot)
+                far_found = jnp.where(hit, rank, far_found)
+                is_far = jnp.where(hit, 1, is_far)
+                rank = rank + jnp.where((group >= 2) == (chip == 1), 1, 0)
+            far_sel[slot] = jnp.minimum(far_found, 2 * CAPACITY - 1)
+            from_far[slot] = is_far
         return carry
 
+    def find_sent(place, carry):
+        found, rank = jnp.int32(0), jnp.int32(0)
+        for number in range(2 * DEVICE_PIECES):
+            leaves = (group_ref[table_at(chip, number)] >= 2) == (chip == 0)
+            found = jnp.where(leaves & (rank == core * CAPACITY + place), number, found)
+            rank = rank + jnp.where(leaves, 1, 0)
+        send_sel[place] = found
+        return carry
+
+    if slim:
+        lax.fori_loop(0, CAPACITY, find_sent, 0)
+        for item in range(2):
+            start_out(item)
+        for item in range(2, 3 + DEPTH):
+            start_near(item)
+        for item in range(2, 2 + DEPTH):
+            start_out(item)
     lax.fori_loop(0, DEVICE_PIECES, find_slot, 0)
 
     def first_token(positions):
@@ -226,9 +285,9 @@
         pass_on(item)
     for item in range(2):
         all_here(item)
-        arrived, placed = (kbuf, vbuf)[item], (kp, vp)[item]
+        placed = (kp, vp)[item]
         for slot in range(DEVICE_PIECES):
-            piece = arrived[sel[slot]]
+            piece = pick(item, slot)
             for head in range(KEY_VALUE_HEADS):
                 placed[head, pl.ds(own_first + slot * PIECE_LENGTH, PIECE_LENGTH), :] = piece[
                     :, head * HEAD_WIDTH : (head + 1) * HEAD_WIDTH
@@ -295,7 +354,9 @@
                     for step in range(1, chips):
                         peer_copy(2 + chunk, step, rep).wait_send()
                     start_out(2 + chunk + DEPTH)
-                    start_near(2 + chunk + DEPTH)
+                    ahead = chunk + DEPTH + (1 if slim else 0)
+                    if ahead < CHUNKS:
+                        start_near(2 + ahead)
 
         @pl.when(count == 1)
         def _():
@@ -312,7 +373,7 @@
             def _():
                 all_here(2 + chunk)
                 for slot in range(DEVICE_PIECES):
-                    qsel[slot] = qbufs[chunk][sel[slot]]
+                    qsel[slot] = pick(2 + chunk, slot)
 
         @pl.when(count >= 1)
         def _():
@@ -345,12 +406,11 @@
                 halo_copy(which, distance).wait_send()
 
 
-def shards(queries, keys, values, doc_lengths, dest_group, dest_slot):
-    groups = lax.axis_size("rep")
-    shard_count = lax.axis_size("sp")
+def gathered_attention(slim, groups, shard_count, operands):
+    queries, keys, values, doc_lengths, dest_group, dest_slot = operands
     chips = groups // 2
     halo = shard_count // 4
-    pieces = groups * DEVICE_PIECES
+    pieces = (2 if slim else groups) * DEVICE_PIECES
     items = CHUNKS + 2
     key_rows = (halo + 1) * BLOCK
     window = halo * BLOCK + HALF_ROWS
@@ -358,16 +418,20 @@
     smem = pl.BlockSpec(memory_space=pltpu.SMEM)
     hbm = pl.BlockSpec(memory_space=pl.ANY)
     dma = pltpu.SemaphoreType.DMA
-    scratch = [pltpu.VMEM((pieces, PIECE_LENGTH, CHUNK), jnp.bfloat16) for _ in range(CHUNKS)]
+    widths = [wide] * 2 + [CHUNK] * CHUNKS
+    scratch = []
+    for count in (pieces, 2 * CAPACITY, CAPACITY) if slim else (pieces,):
+        scratch += [pltpu.VMEM((count, PIECE_LENGTH, width), jnp.bfloat16) for width in widths]
     scratch += [
-        pltpu.VMEM((pieces, PIECE_LENGTH, wide), jnp.bfloat16),
-        pltpu.VMEM((pieces, PIECE_LENGTH, wide), jnp.bfloat16),
         pltpu.VMEM((KEY_VALUE_HEADS, key_rows, HEAD_WIDTH), jnp.bfloat16),
         pltpu.VMEM((KEY_VALUE_HEADS, key_rows, HEAD_WIDTH), jnp.bfloat16),
         pltpu.VMEM((BLOCK, window), jnp.float32),
         pltpu.VMEM((DEVICE_PIECES, PIECE_LENGTH, CHUNK), jnp.bfloat16),
         pltpu.VMEM((2, BLOCK, CHUNK), jnp.bfloat16),
         pltpu.SMEM((DEVICE_PIECES,), jnp.int32),
+        pltpu.SMEM((DEVICE_PIECES,), jnp.int32),
+        pltpu.SMEM((DEVICE_PIECES,), jnp.int32),
+        pltpu.SMEM((CAPACITY,), jnp.int32),
         dma((items,)),
         dma((items, chips - 1)),
         dma((items, chips - 1)),
@@ -381,7 +445,7 @@
     ]
     work = QUERY_HEADS * BLOCK * window
     return pl.pallas_call(
-        functools.partial(kernel, groups, shard_count, halo),
+        functools.partial(kernel, groups, shard_count, halo, slim),
         out_shape=jax.ShapeDtypeStruct(queries.shape, jnp.bfloat16),
         in_specs=[smem, smem, smem, hbm, hbm, hbm],
         out_specs=hbm,
@@ -392,7 +456,7 @@
             transcendentals=work,
         ),
         compiler_params=pltpu.CompilerParams(
-            collective_id=0, has_side_effects=True, vmem_limit_bytes=56 * 1024 * 1024
+            collective_id=1 if slim else 0, has_side_effects=True, vmem_limit_bytes=56 * 1024 * 1024
         ),
     )(
         doc_lengths,
@@ -402,6 +466,19 @@
         keys.reshape(DEVICE_PIECES, PIECE_LENGTH, wide),
         values.reshape(DEVICE_PIECES, PIECE_LENGTH, wide),
     )
+
+
+def shards(*operands):
+    groups = lax.axis_size("rep")
+    shard_count = lax.axis_size("sp")
+    whole = functools.partial(gathered_attention, False, groups, shard_count)
+    if groups != 4:
+        return whole(operands)
+    target_chip = operands[4].reshape(2, 2, shard_count, DEVICE_PIECES) // 2
+    leaves = target_chip != jnp.arange(2)[:, None, None, None]
+    fits = jnp.all(jnp.sum(leaves, axis=(1, 3)) <= 2 * CAPACITY)
+    slim = functools.partial(gathered_attention, True, groups, shard_count)
+    return lax.cond(fits, slim, whole, operands)
 
 
 def solution(mesh):

time: 134 us -> 117 us (0.87)
  Pallas kernels: 128 us -> 112 us
  local copies, waits for them, and re-layouts: 4.64 us -> 2.77 us
    pallas_call x1, Pallas kernels: 128 us -> 112 us  [gathered_attention(): pl.pallas_call(functools.partial(kernel, groups, shard_count, halo, slim)...]
    unnamed x1, local copies, waits for them, and re-layouts: 4.64 us -> 2.02 us
where the time goes in v2:
time: 117 us; the launch traced here: 116 us
  Pallas kernels  112 us (96%)
  local copies, waits for them, and re-layouts  2.77 us (2%)
    pallas_call x1, Pallas kernels, gathered_attention(): pl.pallas_call(functools.partial(kernel, groups, shard_count, halo, slim)...  112 us

profile of v2, /device:TPU:10, one launch (start us, length us, event | category | flops | bytes accessed | tf_op | source)
XLA Modules:
  0.0 116.4 jit_solution(11811462986865236432)
XLA Ops:
  0.0 0.8 reshape.21
  0.8 0.2 convert_reduce_fusion
  0.9 0.6 compare_reduce_fusion
  2.2 112.1 %conditional.1 = (bf16[256,8192]{1,0:T(8,128)(2,1)S(1)}) conditional(s32[]{:T(128)} %convert_element_type.7, (bf16[256,8192]{1,0:T(8,128)(2,1)}, bf16[256,1024]{1,0:T(8,128)(2,1)}, bf16[256,1024]{1,0:T(8,128)(2,1)}, s32[1,16]{1,0:T(1,128)}, s32[4,64]{1,0:T(4,128)}, /*index=5*/s32[4,64]{1,0:T(4,128)}) %tuple.11, (bf16[256,8192]{1,0:T(8,128)(2,1)}, ...), branch_computations={%region_2.3_spmd, %region_3.4_spmd} | conditional | flops 5368709120 | bytes 9437192 | solution.py:481
  2.2 112.1 %branch_1_fun.1 = bf16[256,8192]{1,0:T(8,128)(2,1)S(1)} custom-call(s32[1,16]{1,0:T(1,128)} %get-tuple-element.38.lengths_ref, s32[4,64]{1,0:T(4,128)} %get-tuple-element.39.group_ref, s32[4,64]{1,0:T(4,128)} %get-tuple-element.40.slot_ref, bf16[8,32,8192]{2,1,0:T(8,128)(2,1)} %bitcast.7, bf16[8,32,1024]{2,1,0:T(8,128)(2,1)} %bitcast.9, ...), custom_call_target="tpu_custom_call" | custom-call | flops 5368709120 | bytes 9437184 | tf_op jit(solution)/shard_map/cond/branch_1_fun/pallas_call | solution.py:447
  114.4 2.0 %copy.12 = bf16[256,8192]{1,0:T(8,128)(2,1)} copy(bf16[256,8192]{1,0:T(8,128)(2,1)S(1)} %get-tuple-element.44) | data formatting | bytes 8388608

commit v3 on v2

--- a/solution.py
+++ b/solution.py
@@ -19,6 +19,8 @@
 BLOCK = DEVICE_PIECES * PIECE_LENGTH
 HALF_PIECES = 4
 HALF_ROWS = HALF_PIECES * PIECE_LENGTH
+PARTS = 4
+PART_HEADS = KEY_VALUE_HEADS // PARTS
 CAPACITY = 6
 DEPTH = 3
 
@@ -166,13 +168,14 @@
             piece = jnp.where(from_far[slot] == 1, far[item][far_sel[slot]], piece)
         return piece
 
-    def halo_copy(which, distance):
+    def halo_copy(which, distance, part):
         placed = (kp, vp)[which]
+        heads = pl.ds(part * PART_HEADS, PART_HEADS)
         return pltpu.make_async_remote_copy(
-            src_ref=placed.at[:, pl.ds(own_first, BLOCK), :],
-            dst_ref=placed.at[:, pl.ds((halo - distance) * BLOCK, BLOCK), :],
-            send_sem=halo_send.at[which, distance - 1],
-            recv_sem=halo_recv.at[which, distance - 1],
+            src_ref=placed.at[heads, pl.ds(own_first, BLOCK), :],
+            dst_ref=placed.at[heads, pl.ds((halo - distance) * BLOCK, BLOCK), :],
+            send_sem=halo_send.at[which, distance - 1, part],
+            recv_sem=halo_recv.at[which, distance - 1, part],
             device_id={"sp": lax.rem(shard + distance, shard_count)},
             device_id_type=MESH,
         )
@@ -292,11 +295,13 @@
                 placed[head, pl.ds(own_first + slot * PIECE_LENGTH, PIECE_LENGTH), :] = piece[
                     :, head * HEAD_WIDTH : (head + 1) * HEAD_WIDTH
                 ]
+    for part in range(PARTS):
         for distance in range(1, halo + 1):
 
             @pl.when(shard + distance < shard_count)
             def _():
-                halo_copy(item, distance).start()
+                for which in range(2):
+                    halo_copy(which, distance, part).start()
 
     factor = math.log2(math.e) / math.sqrt(HEAD_WIDTH)
 
@@ -358,14 +363,16 @@
                     if ahead < CHUNKS:
                         start_near(2 + ahead)
 
-        @pl.when(count == 1)
-        def _():
-            for distance in range(1, halo + 1):
-
-                @pl.when(shard >= distance)
-                def _():
-                    for which in range(2):
-                        halo_copy(which, distance).wait_recv()
+        for part in range(PARTS):
+
+            @pl.when(count == 1 + part * PART_HEADS)
+            def _():
+                for distance in range(1, halo + 1):
+
+                    @pl.when(shard >= distance)
+                    def _():
+                        for which in range(2):
+                            halo_copy(which, distance, part).wait_recv()
 
         for chunk in range(CHUNKS):
 
@@ -403,7 +410,8 @@
         @pl.when(shard + distance < shard_count)
         def _():
             for which in range(2):
-                halo_copy(which, distance).wait_send()
+                for part in range(PARTS):
+                    halo_copy(which, distance, part).wait_send()
 
 
 def gathered_attention(slim, groups, shard_count, operands):
@@ -439,8 +447,8 @@
         dma((items,)),
         dma((items, chips - 1)),
         dma((items, chips - 1)),
-        dma((2, halo)),
-        dma((2, halo)),
+        dma((2, halo, PARTS)),
+        dma((2, halo, PARTS)),
         dma((2,)),
     ]
     work = QUERY_HEADS * BLOCK * window

time: 117 us -> 107 us (0.915)
  Pallas kernels: 112 us -> 101 us
    pallas_call x1, Pallas kernels: 112 us -> 101 us  [gathered_attention(): pl.pallas_call(functools.partial(kernel, groups, shard_count, halo, slim)...]
where the time goes in v3:
time: 107 us; the launch traced here: 106 us
  Pallas kernels  101 us (94%)
  local copies, waits for them, and re-layouts  2.77 us (3%)
    pallas_call x1, Pallas kernels, gathered_attention(): pl.pallas_call(functools.partial(kernel, groups, shard_count, halo, slim)...  101 us

profile of v3, /device:TPU:10, one launch (start us, length us, event | category | flops | bytes accessed | tf_op | source)
XLA Modules:
  0.0 105.5 jit_solution(6060329430356592110)
XLA Ops:
  0.0 0.8 reshape.21
  0.8 0.2 convert_reduce_fusion
  0.9 0.6 compare_reduce_fusion
  2.2 101.3 %conditional.1 = (bf16[256,8192]{1,0:T(8,128)(2,1)S(1)}) conditional(s32[]{:T(128)} %convert_element_type.7, (bf16[256,8192]{1,0:T(8,128)(2,1)}, bf16[256,1024]{1,0:T(8,128)(2,1)}, bf16[256,1024]{1,0:T(8,128)(2,1)}, s32[1,16]{1,0:T(1,128)}, s32[4,64]{1,0:T(4,128)}, /*index=5*/s32[4,64]{1,0:T(4,128)}) %tuple.11, (bf16[256,8192]{1,0:T(8,128)(2,1)}, ...), branch_computations={%region_2.3_spmd, %region_3.4_spmd} | conditional | flops 5368709120 | bytes 9437192 | solution.py:489
  2.2 101.3 %branch_1_fun.1 = bf16[256,8192]{1,0:T(8,128)(2,1)S(1)} custom-call(s32[1,16]{1,0:T(1,128)} %get-tuple-element.38.lengths_ref, s32[4,64]{1,0:T(4,128)} %get-tuple-element.39.group_ref, s32[4,64]{1,0:T(4,128)} %get-tuple-element.40.slot_ref, bf16[8,32,8192]{2,1,0:T(8,128)(2,1)} %bitcast.7, bf16[8,32,1024]{2,1,0:T(8,128)(2,1)} %bitcast.9, ...), custom_call_target="tpu_custom_call" | custom-call | flops 5368709120 | bytes 9437184 | tf_op jit(solution)/shard_map/cond/branch_1_fun/pallas_call | solution.py:455
  103.5 2.0 %copy.12 = bf16[256,8192]{1,0:T(8,128)(2,1)} copy(bf16[256,8192]{1,0:T(8,128)(2,1)S(1)} %get-tuple-element.44) | data formatting | bytes 8388608
